TPU v7x, 512 devices: a whole 4x4x16 slice. The times are simulated.
512 devices in a mesh: pipe: 16 (over x, y), tensor: 32 (over z, core).
Axes of the slice: x: 4, y: 4, z: 16, core: 2. Of those that a mesh axis runs over, the one named last changes fastest.
Arguments:
- hidden: bfloat16 [512, 16384], P('pipe', 'tensor'), may hold values from -18 to 18
- head_weight: bfloat16 [73728, 16384], P(('pipe', 'tensor')), may hold values from -0.703125 to 0.703125
- shares: int32 [16], replicated, may hold values from 1 to 4608, 64000 in all
- targets: int32 [512], replicated, may hold values from 0 to 63999
Outputs:
- max_logit: float32 [512], P('pipe')
- log_total: float32 [512], P('pipe')
- target_logprob: float32 [512], P('pipe')
Inputs may be any that keep to these rules, and one draw needn't show every extreme that they name: Each section owns at least one word; the shares sum to 64000; some section owns exactly 4608.
All inputs are finite; a program needn't handle non-finite values.
Results may differ from a plain program's by a relative error of at most 0.0003.
Values may be sent and summed in bfloat16 or wider, within the bound.
A program may use at most 64 MiB of HBM per device.

v0:
```python
import jax
import jax.numpy as jnp
from jax import lax
from jax.sharding import PartitionSpec as P

very_negative = -1e30


def project_rows(left, right):
    return lax.dot_general(
        left, right, (((1,), (1,)), ((), ())), preferred_element_type=jnp.float32
    )


def local(hidden, head_weight, shares, targets):
    sections = lax.axis_size("pipe")
    members = lax.axis_size("tensor")
    section = lax.axis_index("pipe")
    member = lax.axis_index("tensor")
    slots = head_weight.shape[0]
    features = lax.all_gather(hidden, "tensor", axis=1, tiled=True)
    logits = project_rows(lax.all_gather(features, "pipe", axis=0, tiled=True), head_weight)
    section_ids = jnp.arange(sections, dtype=jnp.int32)
    own_share = jnp.sum(jnp.where(section_ids == section, shares, 0))
    offset = jnp.sum(jnp.where(section_ids < section, shares, 0))
    position = jnp.arange(slots, dtype=jnp.int32) * members + member
    live = position < own_share
    word = offset + position
    hit = live[None, :] & (word[None, :] == targets[:, None])
    local_pick = jnp.sum(jnp.where(hit, logits, 0.0), axis=1)
    local_top = jnp.max(jnp.where(live[None, :], logits, very_negative), axis=1)
    top = lax.pmax(local_top, ("pipe", "tensor"))
    local_total = jnp.sum(jnp.where(live[None, :], jnp.exp(logits - top[:, None]), 0.0), axis=1)
    total, picked = lax.psum((local_total, local_pick), ("pipe", "tensor"))
    log_total = top + jnp.log(total)
    row_count = hidden.shape[0]
    begin = section * row_count
    own_top = lax.dynamic_slice_in_dim(top, begin, row_count, 0)
    own_log = lax.dynamic_slice_in_dim(log_total, begin, row_count, 0)
    own_pick = lax.dynamic_slice_in_dim(picked, begin, row_count, 0)
    return (own_top, own_log, own_pick - own_log)


def solution(mesh):
    in_specs = (P("pipe", "tensor"), P(("pipe", "tensor"), None), P(), P())
    out_specs = (P("pipe"), P("pipe"), P("pipe"))
    return jax.shard_map(local, mesh=mesh, in_specs=in_specs, out_specs=out_specs, check_vma=False)
```

profile of v0, /device:TPU:1, one launch (start us, length us, event | category | flops | bytes accessed | tf_op | source)
XLA Modules:
  0.0 436.5 jit_solution(597325643072326438)
XLA Ops:
  7.2 0.0 copy-start
  7.2 0.0 all-gather.3.cloned.1.call-start
  7.2 0.7 all-gather.3.cloned.1.call-update
  7.9 0.0 all-gather.5.cloned.1.call-start
  8.0 78.6 %all-gather.3.cloned.1.call-done = bf16[32,16384]{1,0:T(8,128)(2,1)} async-done(((bf16[32,512]{1,0:T(8,128)(2,1)}), bf16[32,16384]{1,0:T(8,128)(2,1)}) %all-gather.3.cloned.1.call-update) | async-done | bytes 1048592 | tf_op jit(solution)/shard_map/all_gather | solution.py:21
  86.6 0.0 all-gather.5.cloned.1.call-update
  86.6 1.3 fusion.3
  87.9 0.7 fusion.1
  88.6 0.7 fusion
  89.2 123.8 %all-gather.5.cloned.1.call-done = bf16[512,16384]{1,0:T(8,128)(2,1)} async-done(((bf16[32,16384]{1,0:T(8,128)(2,1)}), bf16[512,16384]{1,0:T(8,128)(2,1)}) %all-gather.5.cloned.1.call-update) | async-done | bytes 16777232 | tf_op jit(solution)/shard_map/all_gather | solution.py:22
  213.0 10.7 %select_reduce_fusion.2 = (f32[512]{0:T(512)S(1)}, f32[512,144]{0,1:T(8,128)S(1)}) fusion(pred[144]{0:T(512)(128)(4,1)S(1)} %fusion.1, bf16[512,16384]{1,0:T(8,128)(2,1)} %all-gather.5.cloned.1.call-done, bf16[144,16384]{1,0:T(8,128)(2,1)} %param.5), kind=kOutput, calls=%fused_computation.2 | convolution fusion | flops 2416066048 | bytes 21792912 | tf_op jit(solution)/shard_map/dot_general | solution.py:10
  223.7 104.2 %pmax.7 = f32[512]{0:T(512)S(1)} all-reduce(f32[512]{0:T(512)S(1)} %get-tuple-element.11), channel_id=1, replica_groups=mesh['pipe'=16,'tensor'=32] {'pipe','tensor'}, use_global_device_ids=true, to_apply=%region_2.3 | all-reduce | flops 512 | bytes 4096 | tf_op jit(solution)/shard_map/pmax | solution.py:32
  327.9 0.0 copy-done
  327.9 0.2 select_reduce_fusion
  328.1 100.3 %all-reduce = (f32[512]{0:T(512)S(1)}, f32[512]{0:T(512)S(1)}) all-reduce(f32[512]{0:T(512)S(1)} %get-tuple-element.4, f32[512]{0:T(512)S(1)} %get-tuple-element.3), channel_id=1, replica_groups=mesh['pipe'=16,'tensor'=32] {'pipe','tensor'}, use_global_device_ids=true, to_apply=%region_4.5 | all-reduce | flops 1024 | bytes 8192 | tf_op jit(solution)/shard_map/psum | solution.py:34
  428.5 0.6 dynamic_slice.9
  429.0 0.6 dynamic-slice_subtract_fusion
  (1 shorter events, 0.0 us)
Async XLA Ops:
  7.2 320.8 %copy-start = (s32[512]{0:T(512)S(1)}, s32[512]{0:T(512)}, u32[]{:S(2)}) copy-start(s32[512]{0:T(512)} %param.7) | copy-start | bytes 6148
  7.2 79.4 %all-gather.3.cloned.1.call-start = ((), (), s32[]{:S(2)}) async-start(), calls=%async_computation | async-start | bytes 1081344 | tf_op jit(solution)/shard_map/all_gather | solution.py:21
  7.9 205.1 %all-gather.5.cloned.1.call-start = ((), (), s32[]{:S(2)}) async-start(), calls=%async_computation.1 | async-start | bytes 17825792 | tf_op jit(solution)/shard_map/all_gather | solution.py:22
Sparse Core Ops, SparseCore 0:
  10.2 76.3 all-gather.2
  89.6 123.3 all-gather.4
where the time goes:
time: 437 us; the launch traced here: 436 us
  blocking collectives  205 us (47%)
  waiting for transfers between devices  203 us (46%)
  between operations  14.1 us (3%)
  matrix products  10.7 us (2%)
    all_gather x1, waiting for transfers between devices, local(): lax.all_gather(features, 'pipe', axis=0, tiled=True)  124 us
    pmax x1, blocking collectives, local(): top = lax.pmax(local_top, ('pipe', 'tensor'))  104 us
    psum x1, blocking collectives, local(): total, picked = lax.psum((local_total, local_pick), ('pipe', 'tensor'))  100 us
    all_gather x1, waiting for transfers between devices, local(): features = lax.all_gather(hidden, 'tensor', axis=1, tiled=True)  78.6 us
    dot_general x1, matrix products, project_rows(): lax.dot_general(left, right, (((1,), (1,)), ((), ())), preferred_element_...  10.7 us
  transfers between devices with their start and end apart: 2, of which 2 were waited for; matrix products, arithmetic and copies ran while one was open for 1% of the time, Pallas kernels for 0%

commit v1 on v0

v1 whole, which is shorter than its diff:
```python
import jax
import jax.numpy as jnp
from jax import lax
from jax.experimental import pallas as pl
from jax.experimental.pallas import tpu as pltpu
from jax.sharding import PartitionSpec as P

VERY_NEGATIVE = -1e30
NX, NY, NZ, NQ = 4, 4, 16, 4
ROWS = 32
WIDTH = 512
WIDE = 384
HALF = 16
SLOTS = 144
MESH = pl.DeviceIdType.MESH


def combine(tiles):
    tops = [t[0:1, :] for t in tiles]
    top = tops[0]
    for other in tops[1:]:
        top = jnp.maximum(top, other)
    total = jnp.zeros_like(top)
    pick = jnp.zeros_like(top)
    for t, own in zip(tiles, tops):
        total = total + t[1:2, :] * jnp.exp(own - top)
        pick = pick + t[2:3, :]
    return top, total, pick


def kernel(hidden, weight, shares, targets, top_out, log_out, pick_out,
           X, W, acc, part, st, sx, sy, sz1, sz2, sc,
           a1s, a1r, a2s, a2r, z1s, z1r, z2s, z2r, us, ur, vs, vr, fs, fr, rs, rr,
           ws, wr, wl, hl, ps, pr, ss, sr):
    pipe = lax.axis_index("pipe")
    tensor = lax.axis_index("tensor")
    x, y = pipe // NY, pipe % NY
    z, c = tensor // 2, tensor % 2
    zq, zr = z // NQ, z % NQ

    def at_x(d):
        return (((x + d) % NX) * NY + y, tensor)

    def at_y(d):
        return (x * NY + (y + d) % NY, tensor)

    def at_z(d):
        return (pipe, ((z + d) % NZ) * 2 + c)

    sibling = (pipe, z * 2 + 1 - c)

    def send(src, dst, send_sem, recv_sem, device):
        copy = pltpu.make_async_remote_copy(
            src_ref=src, dst_ref=dst, send_sem=send_sem, recv_sem=recv_sem,
            device_id=device, device_id_type=MESH)
        copy.start()
        sent.append(copy)

    sent = []

    def arrived(ref, sem):
        pltpu.make_async_copy(ref, ref, sem).wait()

    own_block = pltpu.make_async_copy(hidden, X.at[zq, zr, x, y], hl)
    own_block.start()

    def own_weight(k):
        col = pl.multiple_of((2 * k + c) * WIDTH, WIDTH)
        return pltpu.make_async_copy(
            weight.at[:, pl.ds(col, WIDTH)], W.at[k, pl.ds(0, SLOTS), :], wl.at[k])

    def other_weight(k):
        col = pl.multiple_of((2 * k + 1 - c) * WIDTH, WIDTH)
        return pltpu.make_async_remote_copy(
            src_ref=weight.at[:, pl.ds(col, WIDTH)],
            dst_ref=W.at[k, pl.ds(SLOTS, SLOTS), :],
            send_sem=ws.at[k], recv_sem=wr.at[k], device_id=sibling, device_id_type=MESH)

    barrier = pltpu.get_barrier_semaphore()
    greet = [at_x(1), at_x(2), at_x(3), at_y(1), at_y(2), at_y(3), sibling]
    greet += [at_z(d) for d in (1, 2, 4, 8, 12, 14, 15)]
    for device in greet:
        pl.semaphore_signal(barrier, inc=1, device_id=device, device_id_type=MESH)
    pl.semaphore_wait(barrier, len(greet))

    mine = X.at[zq, zr, x, y]
    for i, d in enumerate((4, 12, 8)):
        send(hidden.at[:, pl.ds(0, WIDE)], mine.at[:, pl.ds(0, WIDE)],
             z1s.at[i], z1r.at[i], at_z(d))
    for i, d in enumerate((1, 3, 2)):
        send(hidden.at[:, pl.ds(WIDE, WIDTH - WIDE)], mine.at[:, pl.ds(WIDE, WIDTH - WIDE)],
             a1s.at[i], a1r.at[i], at_x(d))

    @pl.loop(0, NZ)
    def _(k):
        other_weight(k).start()

    @pl.loop(0, NZ)
    def _(k):
        own_weight(k).start()

    own_block.wait()
    for i in range(3):
        arrived(X.at[zq, zr, x, y, :, pl.ds(WIDE, WIDTH - WIDE)], a1r.at[i])
    line = X.at[zq, zr, :, y, :, pl.ds(WIDE, WIDTH - WIDE)]
    for i, d in enumerate((1, 3, 2)):
        send(line, line, a2s.at[i], a2r.at[i], at_y(d))

    for i in range(3):
        arrived(mine.at[:, pl.ds(0, WIDE)], z1r.at[i])
    line = X.at[:, zr, x, y, :, pl.ds(0, WIDE)]
    for i, d in enumerate((1, 15, 2)):
        send(line, line, z2s.at[i], z2r.at[i], at_z(d))

    for i in range(3):
        arrived(X.at[zq, zr, :, y, :, pl.ds(WIDE, WIDTH - WIDE)], a2r.at[i])

    def slab(d, begin, count):
        at = (z + d) % NZ
        return X.at[at // NQ, at % NQ, pl.ds(begin, count), :, :, pl.ds(WIDE, WIDTH - WIDE)]

    def ring(step):
        begin, count = ((0, 4), (0, 4)) if step < 7 else ((0, 2), (2, 2))
        if step == 7:
            begin, count = (0, 2), (2, 2)
        else:
            begin, count = (0, 0), (4, 4)
        up, down = slab(NZ - step, begin[0], count[0]), slab(step, begin[1], count[1])
        send(up, up, rs.at[0, step], rr.at[0, step], at_z(1))
        send(down, down, rs.at[1, step], rr.at[1, step], at_z(15))

    def ring_wait(step):
        if step == 7:
            begin, count = (0, 2), (2, 2)
        else:
            begin, count = (0, 0), (4, 4)
        arrived(slab(NZ - step - 1, begin[0], count[0]), rr.at[0, step])
        arrived(slab(step + 1, begin[1], count[1]), rr.at[1, step])

    ring(0)

    for i in range(3):
        arrived(X.at[:, zr, x, y, :, pl.ds(0, WIDE)], z2r.at[i])

    def column(part_id, du, dv, q0=0, nq=NQ):
        cx, cy = ((x + du) % NX, (y + dv) % NY) if part_id == 0 else ((x + dv) % NX, (y + du) % NY)
        return X.at[pl.ds(q0, nq), :, cx, cy, pl.ds(part_id * HALF, HALF), pl.ds(0, WIDE)]

    def along_u(part_id, d):
        return at_x(d) if part_id == 0 else at_y(d)

    def along_v(part_id, d):
        return at_y(d) if part_id == 0 else at_x(d)

    hops = (0, 3, 1, 2)

    def direct(k):
        for q in range(2):
            block = column(q, hops[k], 0)
            for i, d in enumerate((1, 3)):
                send(block, block, vs.at[q, k, i], vr.at[q, k, i], along_v(q, d))

    def forward(k):
        for q in range(2):
            arrived(column(q, hops[k], 3), vr.at[q, k, 0])
            block = column(q, hops[k], 3, 0, 2)
            send(block, block, fs.at[q, k, 0], fr.at[q, k, 0], along_v(q, 1))
            arrived(column(q, hops[k], 1), vr.at[q, k, 1])
            block = column(q, hops[k], 1, 2, 2)
            send(block, block, fs.at[q, k, 1], fr.at[q, k, 1], along_v(q, 3))

    for q in range(2):
        block = column(q, 0, 0)
        for i, d in enumerate((1, 3, 2)):
            send(block, block, us.at[q, i], ur.at[q, i], along_u(q, d))
    direct(0)

    def u_wait(k):
        for q in range(2):
            arrived(column(q, hops[k], 0), ur.at[q, k - 1])

    ring_wait(0)
    ring(1)
    u_wait(1)
    direct(1)
    ring_wait(1)
    ring(2)
    u_wait(2)
    direct(2)
    ring_wait(2)
    ring(3)
    u_wait(3)
    direct(3)
    ring_wait(3)
    ring(4)
    forward(0)
    ring_wait(4)
    ring(5)
    forward(1)
    ring_wait(5)
    ring(6)
    forward(2)
    ring_wait(6)
    ring(7)
    forward(3)
    ring_wait(7)
    for k in range(4):
        for q in range(2):
            arrived(column(q, hops[k], 2, 0, 2), fr.at[q, k, 0])
            arrived(column(q, hops[k], 2, 2, 2), fr.at[q, k, 1])

    @pl.loop(0, NZ)
    def _(k):
        own_weight(k).wait()
        other_weight(k).wait()

    acc[...] = jnp.zeros_like(acc)

    @pl.loop(0, NZ)
    def _(k):
        rows = X[k // NQ, k % NQ].reshape(NX * NY * ROWS, WIDTH)
        acc[...] += lax.dot_general(
            W[k], rows, (((1,), (1,)), ((), ())), preferred_element_type=jnp.float32)

    swap = pltpu.make_async_remote_copy(
        src_ref=acc.at[pl.ds(SLOTS, SLOTS), :], dst_ref=part, send_sem=ps, recv_sem=pr,
        device_id=sibling, device_id_type=MESH)
    swap.start()

    own_share = jnp.int32(0)
    offset = jnp.int32(0)
    for s in range(NX * NY):
        own_share = own_share + jnp.where(s == pipe, shares[s], 0)
        offset = offset + jnp.where(s < pipe, shares[s], 0)
    position = lax.broadcasted_iota(jnp.int32, (SLOTS, NX * NY * ROWS), 0) * (2 * NZ) + tensor
    live = position < own_share
    hit = live & (position + offset == targets[...])
    swap.wait()
    logits = acc[pl.ds(0, SLOTS), :] + part[...]
    top = jnp.max(jnp.where(live, logits, VERY_NEGATIVE), axis=0, keepdims=True)
    total = jnp.sum(jnp.where(live, jnp.exp(logits - top), 0.0), axis=0, keepdims=True)
    pick = jnp.sum(jnp.where(hit, logits, 0.0), axis=0, keepdims=True)

    def put(ref, values):
        for i, v in enumerate(values):
            ref[pl.ds(i, 1), :] = v

    st[...] = jnp.zeros_like(st)
    for k in range(NX):
        for i, v in enumerate((top, total, pick)):
            st[k, pl.ds(i, 1), :] = v[:, 128 * k:128 * (k + 1)]

    for i, d in enumerate((1, 3, 2)):
        send(st.at[(x + d) % NX], sx.at[x], ss.at[0, i], sr.at[0, i], at_x(d))
    sx[x] = st[x]
    for i in range(3):
        arrived(sx.at[0], sr.at[0, i])

    def stage(n, here, buf, me, peers):
        buf[me] = jnp.zeros((8, 128), jnp.float32)
        put(buf.at[me], here)
        for i, device in enumerate(peers):
            send(buf.at[me], buf.at[me], ss.at[n, i], sr.at[n, i], device)
        for i in range(len(peers)):
            arrived(buf.at[0], sr.at[n, i])
        return combine([buf[i] for i in range(buf.shape[0])])

    here = combine([sx[i] for i in range(NX)])
    here = stage(1, here, sy, y, [at_y(1), at_y(3), at_y(2)])
    here = stage(2, here, sz1, zq, [at_z(4), at_z(12), at_z(8)])
    here = stage(3, here, sz2, zr, [at_z(1), at_z(15), at_z(2)])
    top, total, pick = stage(4, here, sc, c, [sibling])
    log_total = top + jnp.log(total)
    for out, v in ((top_out, top), (log_out, log_total), (pick_out, pick - log_total)):
        own = jnp.zeros((1, ROWS), jnp.float32)
        for k in range(NY):
            own = jnp.where(y == k, v[:, ROWS * k:ROWS * (k + 1)], own)
        out[...] = own
    for copy in sent:
        copy.wait_send()


def local(hidden, head_weight, shares, targets):
    dma = pltpu.SemaphoreType.DMA
    rows = NX * NY * ROWS
    tile = lambda n: pltpu.VMEM((n, 8, 128), jnp.float32)
    pairs = [(3,), (3,), (3,), (3,), (2, 3), (2, 4, 2), (2, 4, 2), (2, 8)]
    sems = [dma(s) for s in pairs for _ in range(2)]
    outs = pl.pallas_call(
        kernel,
        out_shape=[jax.ShapeDtypeStruct((1, ROWS), jnp.float32)] * 3,
        in_specs=[
            pl.BlockSpec(memory_space=pl.ANY),
            pl.BlockSpec(memory_space=pl.ANY),
            pl.BlockSpec(memory_space=pltpu.SMEM),
            pl.BlockSpec(memory_space=pltpu.VMEM),
        ],
        out_specs=[pl.BlockSpec(memory_space=pltpu.VMEM)] * 3,
        scratch_shapes=[
            pltpu.VMEM((NQ, NZ // NQ, NX, NY, ROWS, WIDTH), jnp.bfloat16),
            pltpu.VMEM((NZ, 2 * SLOTS, WIDTH), jnp.bfloat16),
            pltpu.VMEM((2 * SLOTS, rows), jnp.float32),
            pltpu.VMEM((SLOTS, rows), jnp.float32),
            tile(NX), tile(NX), tile(NY), tile(NQ), tile(NQ), tile(2),
            *sems,
            dma((NZ,)), dma((NZ,)), dma((NZ,)), dma(()), dma(()), dma(()),
            dma((5, 3)), dma((5, 3)),
        ],
        compiler_params=pltpu.CompilerParams(
            collective_id=0, has_side_effects=True, vmem_limit_bytes=48 * 1024 * 1024),
        cost_estimate=pl.CostEstimate(
            flops=2 * rows * SLOTS * 2 * NZ * WIDTH, bytes_accessed=22 * 1024 * 1024,
            transcendentals=rows * SLOTS),
    )(hidden, head_weight, shares, targets.reshape(1, rows))
    return tuple(o.reshape(ROWS) for o in outs)


def solution(mesh):
    in_specs = (P("pipe", "tensor"), P(("pipe", "tensor"), None), P(), P())
    out_specs = (P("pipe"), P("pipe"), P("pipe"))
    return jax.shard_map(local, mesh=mesh, in_specs=in_specs, out_specs=out_specs, check_vma=False)
```

time: 437 us -> 109 us (0.25)
  blocking collectives: 205 us -> 0 us
  waiting for transfers between devices: 203 us -> 0 us
  Pallas kernels: 0 us -> 102 us
  between operations: 14.1 us -> 0.65 us
  matrix products: 10.7 us -> 0 us
  local copies, waits for them, and re-layouts: 0.59 us -> 5.96 us
    all_gather x2 -> x0, waiting for transfers between devices: 202 us -> none  [the longest x1 124 us: local(): lax.all_gather(features, 'pipe', axis=0, tiled=True)]
    pmax x1 -> x0, blocking collectives: 104 us -> none  [local(): top = lax.pmax(local_top, ('pipe', 'tensor'))]
    pallas_call x0 -> x1, Pallas kernels: none -> 102 us  [local(): pl.pallas_call(kernel, out_shape=[jax.ShapeDtypeStruct((1, ROWS), jnp.flo...]
    psum x1 -> x0, blocking collectives: 100 us -> none  [local(): total, picked = lax.psum((local_total, local_pick), ('pipe', 'tensor'))]
    dot_general x1 -> x0, matrix products: 10.7 us -> none  [project_rows(): lax.dot_general(left, right, (((1,), (1,)), ((), ())), preferred_element_...]
    unnamed x2 -> x11, local copies, waits for them, and re-layouts: 0.01 us -> 5.96 us
  transfers between devices with their start and end apart: 2 -> 0, of which waited for: 2 -> 0; matrix products, arithmetic and copies ran while one was open for 1% -> 0% of each run, Pallas kernels for 0% -> 0%
where the time goes in v1:
time: 109 us
  Pallas kernels  102 us (94%)
  local copies, waits for them, and re-layouts  5.96 us (5%)
    pallas_call x1, Pallas kernels, local(): pl.pallas_call(kernel, out_shape=[jax.ShapeDtypeStruct((1, ROWS), jnp.flo...  102 us
    unnamed x11, local copies, waits for them, and re-layouts  5.96 us

profile of v1, /device:TPU:1, one launch (start us, length us, event | category | flops | bytes accessed | tf_op | source)
XLA Modules:
  0.0 109.1 jit_solution(6073257938252009444)
XLA Ops:
  0.6 0.0 copy-start
  0.6 2.3 %copy-done = bf16[144,16384]{1,0:T(8,128)(2,1)S(1)} copy-done((bf16[144,16384]{1,0:T(8,128)(2,1)S(1)}, bf16[144,16384]{1,0:T(8,128)(2,1)}, u32[]{:S(2)}) %copy-start) | copy-done | bytes 4718616
  3.0 0.0 copy-start.1
  3.0 0.8 copy-done.1
  3.7 0.0 copy-start.2
  3.7 0.7 copy-done.2
  4.4 0.0 copy-start.3
  4.4 0.7 copy-done.3
  5.1 102.5 %shard_map.67 = (f32[1,32]{1,0:T(1,128)S(1)}, f32[1,32]{1,0:T(1,128)S(1)}, f32[1,32]{1,0:T(1,128)S(1)}) custom-call(bf16[32,512]{1,0:T(8,128)(2,1)S(1)} %copy-done.1, bf16[144,16384]{1,0:T(8,128)(2,1)S(1)} %copy-done, s32[16]{0:T(128)S(1)} %copy-done.3, s32[1,512]{1,0:T(1,128)S(1)} %bitcast.4), custom_call_target="tpu_custom_call" | custom-call | flops 2415919104 | bytes 23068672 | tf_op jit(solution)/shard_map/pallas_call | solution.py:289
  107.6 0.5 copy.10
  108.1 0.5 copy.11
  108.6 0.5 copy.12
Async XLA Ops:
  0.6 2.3 %copy-start = (bf16[144,16384]{1,0:T(8,128)(2,1)S(1)}, bf16[144,16384]{1,0:T(8,128)(2,1)}, u32[]{:S(2)}) copy-start(bf16[144,16384]{1,0:T(8,128)(2,1)} %weight.1) | copy-start | bytes 14155780
  3.0 0.8 copy-start.1
  3.7 0.7 copy-start.2
  4.4 0.7 copy-start.3

commit v2 on v0

v2 whole, which is shorter than its diff:
```python
import jax
import jax.numpy as jnp
from jax import lax
from jax.experimental import pallas as pl
from jax.experimental.pallas import tpu as pltpu
from jax.sharding import PartitionSpec as P

VERY_NEGATIVE = -1e30
NX, NY, NZ = 4, 4, 16
FAR = NZ // 2
ROWS = 32
HALF = 16
WIDTH = 512
WIDE = 384
SLOTS = 144
LANES = 128
MESH = pl.DeviceIdType.MESH
TIMES = dict(z=2.8, o=3.2, v=4.1, v0=6.0, a0=6.5, a=3.4, m=4.2)


def below(s):
    return 2 * s - 1 if s else 0


def above(s):
    return 2 * s


def pair(s):
    if s == 0:
        return 0, 1
    return (2 * s - 1, 2) if s < FAR else (2 * FAR - 1, 1)


def join(v):
    lane = lax.broadcasted_iota(jnp.int32, (1, LANES), 1)
    middle = (lane >= ROWS) & (lane < 2 * ROWS)
    rows = [v[i] for i in range(v.shape[0])]
    top = rows[0]
    for r in rows[1:]:
        top = jnp.maximum(top, r)
    total = jnp.zeros_like(top)
    for r in rows:
        scale = pltpu.roll(jnp.exp(r - top), ROWS, 1)
        total = total + r * jnp.where(middle, scale, 1.0)
    return jnp.where(lane < ROWS, top, total)


def kernel(hidden, weight, shares, targets, out,
           X, W, acc, part, goal, own_sh, pack, sxy, sz, sc,
           zs, zr, a1s, a1r, a2s, a2r, rs, rr, os, orr, vs, vr, fs, fr,
           ws, wr, wl, hl, gl, ps, pr, xs, xr, ts, tr, cs, cr):
    pipe = lax.axis_index("pipe")
    tensor = lax.axis_index("tensor")
    x, y = pipe // NY, pipe % NY
    z, c = tensor // 2, tensor % 2

    def at_xy(dx, dy):
        return (((x + dx) % NX) * NY + (y + dy) % NY, tensor)

    def at_z(d):
        return (pipe, ((z + d) % NZ) * 2 + c)

    sibling = (pipe, z * 2 + 1 - c)
    sent = []

    def send(src, dst, send_sem, recv_sem, device):
        copy = pltpu.make_async_remote_copy(
            src_ref=src, dst_ref=dst, send_sem=send_sem, recv_sem=recv_sem,
            device_id=device, device_id_type=MESH)
        copy.start()
        sent.append(copy)

    def arrived(ref, sem):
        pltpu.make_async_copy(ref, ref, sem).wait()

    def feature_block(j, core):
        step = (j + 1) // 2
        at = jnp.where(j % 2 == 1, z + NZ - step, z + step) % NZ
        return pl.ds(pl.multiple_of((2 * at + core) * WIDTH, WIDTH), WIDTH)

    def own_weight(j):
        return pltpu.make_async_copy(
            weight.at[:, feature_block(j, c)], W.at[j, pl.ds(0, SLOTS), :], wl.at[j])

    def other_weight(j):
        return pltpu.make_async_remote_copy(
            src_ref=weight.at[:, feature_block(j, 1 - c)],
            dst_ref=W.at[j, pl.ds(SLOTS, SLOTS), :],
            send_sem=ws.at[j], recv_sem=wr.at[j], device_id=sibling, device_id_type=MESH)

    barrier = pltpu.get_barrier_semaphore()
    greet = [at_xy(1, 0), at_xy(3, 0), at_xy(0, 1), at_xy(0, 3), at_z(1), at_z(15),
             at_xy(2, 0), at_xy(0, 2), sibling]
    for device in greet:
        pl.semaphore_signal(barrier, inc=1, device_id=device, device_id_type=MESH)
    own_block = pltpu.make_async_copy(hidden, X.at[0, 0, 0], hl)
    own_block.start()
    pl.semaphore_wait(barrier, len(greet))

    wide, narrow = pl.ds(0, WIDE), pl.ds(WIDE, WIDTH - WIDE)
    upper, lower = pl.ds(0, HALF), pl.ds(HALF, HALF)
    both = pl.ds(0, ROWS)

    def z_send(s):
        src_up = hidden.at[:, wide] if s == 1 else X.at[below(s - 1), 0, 0, :, wide]
        src_down = hidden.at[:, wide] if s == 1 else X.at[above(s - 1), 0, 0, :, wide]
        dst_up, dst_down = X.at[below(s), 0, 0, :, wide], X.at[min(above(s), NZ - 1), 0, 0, :, wide]
        if s == FAR:
            src_up, dst_up = src_up.at[upper], dst_up.at[upper]
            src_down, dst_down = src_down.at[lower], dst_down.at[lower]
        send(src_up, dst_up, zs.at[s - 1, 0], zr.at[s - 1, 0], at_z(1))
        send(src_down, dst_down, zs.at[s - 1, 1], zr.at[s - 1, 1], at_z(15))

    def z_wait(s):
        a, b = X.at[below(s), 0, 0, :, wide], X.at[min(above(s), NZ - 1), 0, 0, :, wide]
        if s == FAR:
            a, b = a.at[upper], b.at[lower]
        arrived(a, zr.at[s - 1, 0])
        arrived(b, zr.at[s - 1, 1])

    def o_send(s):
        first, n = pair(s)
        at = pl.ds(first, n)
        if s == 0:
            def src(r):
                return hidden.at[r, wide]

            def dst(a, b, r):
                return X.at[0, a, b, r, wide]
        else:
            def src(r):
                return X.at[at, 0, 0, r, wide]

            def dst(a, b, r):
                return X.at[at, a, b, r, wide]
        plan = [((1, 0), both), ((0, 1), both), ((3, 0), both), ((0, 3), both), ((2, 0), upper), ((0, 2), lower)]
        for i, ((dx, dy), r) in enumerate(plan):
            send(src(r), dst(-dx % NX, -dy % NY, r), os.at[s, i], orr.at[s, i], at_xy(dx, dy))

    def o_wait(s):
        at = pl.ds(*pair(s))
        plan = [((1, 0), both), ((0, 1), both), ((3, 0), both), ((0, 3), both), ((2, 0), upper), ((0, 2), lower)]
        for i, ((dx, dy), r) in enumerate(plan):
            arrived(X.at[at, -dx % NX, -dy % NY, r, wide], orr.at[s, i])

    def v_send(s):
        at, rest = pl.ds(*pair(s)), pl.ds(1, 3)
        for i, d in enumerate((1, 3)):
            send(X.at[at, rest, 0, upper, wide], X.at[at, rest, -d % NY, upper, wide],
                 vs.at[s, 0, i], vr.at[s, 0, i], at_xy(0, d))
            send(X.at[at, 0, rest, lower, wide], X.at[at, -d % NX, rest, lower, wide],
                 vs.at[s, 1, i], vr.at[s, 1, i], at_xy(d, 0))

    def v_wait(s):
        at, rest = pl.ds(*pair(s)), pl.ds(1, 3)
        for i, d in enumerate((1, 3)):
            arrived(X.at[at, rest, -d % NY, upper, wide], vr.at[s, 0, i])
            arrived(X.at[at, -d % NX, rest, lower, wide], vr.at[s, 1, i])

    def f_send(s):
        at = pl.ds(*pair(s))
        for i, d in enumerate((1, 3)):
            h = pl.ds(2 * i, 2)
            send(X.at[at, h, -d % NY, upper, wide], X.at[at, h, 2, upper, wide],
                 fs.at[s, 0, i], fr.at[s, 0, i], at_xy(0, d))
            send(X.at[at, -d % NX, h, lower, wide], X.at[at, 2, h, lower, wide],
                 fs.at[s, 1, i], fr.at[s, 1, i], at_xy(d, 0))

    def f_wait(s):
        at = pl.ds(*pair(s))
        for i in range(2):
            h = pl.ds(2 * i, 2)
            arrived(X.at[at, h, 2, upper, wide], fr.at[s, 0, i])
            arrived(X.at[at, 2, h, lower, wide], fr.at[s, 1, i])

    def a1_send():
        for i, d in enumerate((1, 3, 2)):
            send(hidden.at[:, narrow], X.at[0, -d % NX, 0, :, narrow], a1s.at[i], a1r.at[i], at_xy(d, 0))

    def a2_send():
        for i, d in enumerate((1, 3, 2)):
            arrived(X.at[0, -d % NX, 0, :, narrow], a1r.at[i])
        for i, d in enumerate((1, 3, 2)):
            send(X.at[0, :, 0, :, narrow], X.at[0, :, -d % NY, :, narrow], a2s.at[i], a2r.at[i], at_xy(0, d))

    def a2_wait():
        for i, d in enumerate((1, 3, 2)):
            arrived(X.at[0, :, -d % NY, :, narrow], a2r.at[i])

    def slab(j, h):
        return X.at[j, pl.ds(2 * h, 2), :, :, narrow]

    def ring_send(s, h):
        if s < FAR or h == 0:
            send(slab(below(s - 1), h), slab(below(s), h), rs.at[s - 1, h, 0], rr.at[s - 1, h, 0], at_z(1))
        if s < FAR or h == 1:
            send(slab(above(s - 1), h), slab(min(above(s), NZ - 1), h),
                 rs.at[s - 1, h, 1], rr.at[s - 1, h, 1], at_z(15))

    def ring_wait(s, h):
        if s < FAR or h == 0:
            arrived(slab(below(s), h), rr.at[s - 1, h, 0])
        if s < FAR or h == 1:
            arrived(slab(min(above(s), NZ - 1), h), rr.at[s - 1, h, 1])

    def multiply(s):
        first, n = pair(s)
        for j in range(first, first + n):
            own_weight(j).wait()
            other_weight(j).wait()
        @pl.loop(first, first + n)
        def _(j):
            part_sum = lax.dot_general(
                W[j], X[j].reshape(NX * NY * ROWS, WIDTH),
                (((1,), (1,)), ((), ())), preferred_element_type=jnp.float32)
            if s == 0:
                acc[...] = part_sum
            else:
                acc[...] += part_sum

    events = []

    def add(time, *steps):
        events.append((time, len(events), steps))

    T = TIMES
    z_send(1)
    o_send(0)
    a1_send()

    @pl.loop(0, NZ)
    def _(j):
        other_weight(j).start()
        own_weight(j).start()

    own_block.wait()
    goals = [pltpu.make_async_copy(targets.at[(x + d) % NX], goal.at[d], gl.at[d]) for d in range(NX)]
    share_copy = pltpu.make_async_copy(shares, own_sh, gl.at[NX])
    for g in goals + [share_copy]:
        g.start()

    ring_at = {s: T['a0'] + T['a'] * s for s in range(FAR + 1)}
    add(3.0, a2_send)
    add(T['a0'], a2_wait, lambda: ring_send(1, 0), lambda: ring_send(1, 1))
    for s in range(1, FAR + 1):
        for h in range(2):
            steps = [lambda s=s, h=h: ring_wait(s, h)]
            if s < FAR:
                steps.append(lambda s=s, h=h: ring_send(s + 1, h))
            add(ring_at[s] + (T['a'] / 2) * (h - 1), *steps)
    v_last = 0.0
    for s in range(FAR + 1):
        z_at = T['z'] * s
        if s:
            steps = [lambda s=s: z_wait(s)]
            if s < FAR:
                steps.append(lambda s=s: z_send(s + 1))
            steps.append(lambda s=s: o_send(s))
            add(z_at, *steps)
        o_at = z_at + T['o']
        add(o_at, lambda s=s: o_wait(s), lambda s=s: v_send(s))
        v_at = max(o_at + 2.5, T['v0'] + T['v'] * s)
        add(v_at, lambda s=s: v_wait(s), lambda s=s: f_send(s))
        add(max(v_at + T['m'], ring_at[s] + 0.01), lambda s=s: f_wait(s), lambda s=s: multiply(s))
    for _, _, steps in sorted(events, key=lambda e: e[:2]):
        for step in steps:
            step()

    swap = pltpu.make_async_remote_copy(
        src_ref=acc.at[pl.ds(SLOTS, SLOTS), :], dst_ref=part, send_sem=ps, recv_sem=pr,
        device_id=sibling, device_id_type=MESH)
    swap.start()
    for g in goals + [share_copy]:
        g.wait()
    own_share = jnp.int32(0)
    offset = jnp.int32(0)
    for s in range(NX * NY):
        own_share = own_share + jnp.where(s == pipe, own_sh[s], 0)
        offset = offset + jnp.where(s < pipe, own_sh[s], 0)
    position = lax.broadcasted_iota(jnp.int32, (SLOTS, 1), 0) * (2 * NZ) + tensor
    live = position < own_share
    word = position + offset
    lane = lax.broadcasted_iota(jnp.int32, (1, LANES), 1)
    swap.wait()

    def packed(values, dy):
        top, total, pick = values
        moved = [pltpu.roll(v, (ROWS * (i - dy)) % LANES, 1) if (ROWS * (i - dy)) % LANES else v
                 for i, v in enumerate((top, total, pick))]
        return jnp.where(lane < ROWS, moved[0], jnp.where(lane < 2 * ROWS, moved[1], moved[2]))

    for dx in range(NX):
        cols = pl.ds(dx * LANES, LANES)
        logits = acc[pl.ds(0, SLOTS), cols] + part[:, cols]
        want = goal[dx]
        turned = want
        for k in range(1, NY):
            turned = jnp.where(y == k, pltpu.roll(want, LANES - ROWS * k, 1), turned)
        top = jnp.max(jnp.where(live, logits, VERY_NEGATIVE), axis=0, keepdims=True)
        total = jnp.sum(jnp.where(live, jnp.exp(logits - top), 0.0), axis=0, keepdims=True)
        pick = jnp.sum(jnp.where(live & (word == turned), logits, 0.0), axis=0, keepdims=True)
        for dy in range(NY):
            row = packed((top, total, pick), dy)
            if dx == 0 and dy == 0:
                sxy[0] = row
            else:
                pack[dx * NY + dy] = row
                to = (-dx % NX) * NY + (-dy % NY)
                send(pack.at[dx * NY + dy], sxy.at[to], xs.at[to], xr.at[to], at_xy(dx, dy))
    for i in range(1, NX * NY):
        arrived(sxy.at[i], xr.at[i])
    sz[z] = join(sxy[...])
    for d in (8, 7, 9, 6, 10, 5, 11, 4, 12, 3, 13, 2, 14, 1, 15):
        send(sz.at[z], sz.at[z], ts.at[d], tr.at[d], at_z(d))
    while len(sent) > 15:
        sent.pop(0).wait_send()
    for d in range(1, NZ):
        arrived(sz.at[(z + NZ - d) % NZ], tr.at[d])
    sc[c] = join(sz[...])
    send(sc.at[c], sc.at[c], cs, cr, sibling)
    arrived(sc.at[1 - c], cr)
    row = join(sc[...])
    log_total = pltpu.roll(row, ROWS, 1) + jnp.log(jnp.where((lane >= ROWS) & (lane < 2 * ROWS), row, 1.0))
    out[...] = jnp.where(lane < ROWS, row, jnp.where(
        lane < 2 * ROWS, log_total, row - pltpu.roll(log_total, ROWS, 1)))
    for copy in sent:
        copy.wait_send()


def local(hidden, head_weight, shares, targets):
    dma = pltpu.SemaphoreType.DMA
    rows = NX * NY * ROWS
    n = FAR + 1
    line = lambda k: pltpu.VMEM((k, 1, LANES), jnp.float32)
    pairs = [(FAR, 2), (3,), (3,), (FAR, 2, 2), (n, 6), (n, 2, 2), (n, 2, 2)]
    hbm = pl.BlockSpec(memory_space=pltpu.HBM)
    out = pl.pallas_call(
        kernel,
        out_shape=jax.ShapeDtypeStruct((1, LANES), jnp.float32),
        in_specs=[hbm] * 4,
        out_specs=pl.BlockSpec(memory_space=pltpu.VMEM),
        scratch_shapes=[
            pltpu.VMEM((NZ, NX, NY, ROWS, WIDTH), jnp.bfloat16),
            pltpu.VMEM((NZ, 2 * SLOTS, WIDTH), jnp.bfloat16),
            pltpu.VMEM((2 * SLOTS, rows), jnp.float32),
            pltpu.VMEM((SLOTS, rows), jnp.float32),
            pltpu.VMEM((NX, 1, LANES), jnp.int32),
            pltpu.SMEM((NX * NY,), jnp.int32),
            line(16), line(16), line(NZ), line(2),
            *[dma(s) for s in pairs for _ in range(2)],
            dma((NZ,)), dma((NZ,)), dma((NZ,)), dma(()), dma((NX + 1,)), dma(()), dma(()),
            dma((16,)), dma((16,)), dma((NZ,)), dma((NZ,)), dma(()), dma(()),
        ],
        compiler_params=pltpu.CompilerParams(
            collective_id=0, has_side_effects=True, vmem_limit_bytes=60 * 1024 * 1024),
        cost_estimate=pl.CostEstimate(
            flops=2 * rows * SLOTS * 2 * NZ * WIDTH, bytes_accessed=22 * 1024 * 1024,
            transcendentals=rows * SLOTS),
    )(hidden, head_weight, shares, targets.reshape(NX, 1, LANES))
    return tuple(out[0, ROWS * i:ROWS * (i + 1)] for i in range(3))


def solution(mesh):
    in_specs = (P("pipe", "tensor"), P(("pipe", "tensor"), None), P(), P())
    out_specs = (P("pipe"), P("pipe"), P("pipe"))
    return jax.shard_map(local, mesh=mesh, in_specs=in_specs, out_specs=out_specs, check_vma=False)
```

time: 437 us -> 87.9 us (0.20)
  blocking collectives: 205 us -> 0 us
  waiting for transfers between devices: 203 us -> 0 us
  Pallas kernels: 0 us -> 85.8 us
  between operations: 14.1 us -> 0.64 us
  matrix products: 10.7 us -> 0 us
    all_gather x2 -> x0, waiting for transfers between devices: 202 us -> none  [the longest x1 124 us: local(): lax.all_gather(features, 'pipe', axis=0, tiled=True)]
    pmax x1 -> x0, blocking collectives: 104 us -> none  [local(): top = lax.pmax(local_top, ('pipe', 'tensor'))]
    psum x1 -> x0, blocking collectives: 100 us -> none  [local(): total, picked = lax.psum((local_total, local_pick), ('pipe', 'tensor'))]
    pallas_call x0 -> x1, Pallas kernels: none -> 85.8 us  [local(): pl.pallas_call(kernel, out_shape=jax.ShapeDtypeStruct((1, LANES), jnp.flo...]
    dot_general x1 -> x0, matrix products: 10.7 us -> none  [project_rows(): lax.dot_general(left, right, (((1,), (1,)), ((), ())), preferred_element_...]
  transfers between devices with their start and end apart: 2 -> 0, of which waited for: 2 -> 0; matrix products, arithmetic and copies ran while one was open for 1% -> 0% of each run, Pallas kernels for 0% -> 0%
where the time goes in v2:
time: 87.9 us; the launch traced here: 87.8 us
  Pallas kernels  85.8 us (98%)
  local copies, waits for them, and re-layouts  1.3 us (1%)
    pallas_call x1, Pallas kernels, local(): pl.pallas_call(kernel, out_shape=jax.ShapeDtypeStruct((1, LANES), jnp.flo...  85.8 us

profile of v2, /device:TPU:1, one launch (start us, length us, event | category | flops | bytes accessed | tf_op | source)
XLA Modules:
  0.0 87.8 jit_solution(15038243355613608439)
XLA Ops:
  0.6 85.8 %shard_map.67 = f32[1,128]{1,0:T(1,128)} custom-call(bf16[32,512]{1,0:T(8,128)(2,1)} %hidden.1, bf16[144,16384]{1,0:T(8,128)(2,1)} %weight.1, s32[16]{0:T(128)} %shares.1, s32[4,1,128]{2,1,0:T(1,128)} %bitcast.7), custom_call_target="tpu_custom_call" | custom-call | flops 2415919104 | bytes 23068672 | tf_op jit(solution)/shard_map/pallas_call | solution.py:338
  86.5 1.3 %slice_bitcast_fusion = (f32[32]{0:T(128)}, f32[32]{0:T(128)}, f32[32]{0:T(128)}) fusion(f32[1,128]{1,0:T(1,128)} %shard_map.67), kind=kLoop, calls=%fused_computation | loop fusion | bytes 768 | tf_op jit(solution)/shard_map/squeeze | solution.py:361

commit v3 on v2

v3 whole, which is shorter than its diff:
```python
import math

import jax
import jax.numpy as jnp
from jax import lax
from jax.experimental import pallas as pl
from jax.experimental.pallas import tpu as pltpu
from jax.sharding import PartitionSpec as P

VERY_NEGATIVE = -1e30
NX, NY, NZ = 4, 4, 16
FAR = NZ // 2
ROWS = 32
HALF = 16
WIDTH = 512
WIDE = 384
SLOTS = 144
LANES = 128
MESH = pl.DeviceIdType.MESH
HOP = (1, 1, 1, 1, 1, 1, 1, 1)
PIECES = 8
ORDER = (
    ("z", 1), ("a2",), ("a0",), ("o", 0), ("z", 2), ("r", 1, 1), ("r", 1, 0), ("o", 1), ("z", 3), ("a3",),
    ("v", 0), ("r", 2, 1), ("r", 2, 0), ("o", 2), ("z", 4), ("m", 0), ("r", 1, 5), ("r", 1, 7), ("r", 1, 3),
    ("r", 1, 2), ("r", 1, 4), ("r", 1, 6), ("r", 3, 1), ("r", 3, 0), ("o", 3), ("v", 1), ("z", 5), ("v", 2),
    ("o", 4), ("r", 2, 5), ("r", 2, 7), ("r", 2, 3), ("r", 2, 2), ("r", 2, 4), ("r", 2, 6), ("r", 4, 1), ("r",
    4, 0), ("z", 6), ("r", 3, 5), ("r", 3, 7), ("r", 3, 3), ("m", 1), ("r", 3, 2), ("o", 5), ("r", 3, 4),
    ("v", 3), ("r", 3, 6), ("r", 5, 1), ("r", 5, 0), ("r", 4, 5), ("z", 7), ("r", 4, 7), ("r", 4, 3), ("m",
    2), ("o", 6), ("v", 4), ("r", 4, 2), ("r", 4, 4), ("r", 4, 6), ("r", 6, 1), ("r", 6, 0), ("z", 8), ("r",
    5, 5), ("r", 5, 7), ("r", 5, 3), ("r", 5, 2), ("r", 5, 4), ("m", 3), ("r", 5, 6), ("v", 5), ("r", 7, 1),
    ("o", 7), ("r", 7, 0), ("r", 6, 5), ("r", 6, 7), ("r", 6, 3), ("o", 8), ("r", 6, 2), ("r", 6, 4), ("m",
    4), ("v", 6), ("r", 6, 6), ("r", 8, 1), ("r", 8, 0), ("m", 5), ("r", 7, 5), ("r", 7, 7), ("r", 7, 3),
    ("v", 7), ("r", 7, 2), ("r", 7, 4), ("v", 8), ("r", 7, 6), ("m", 6), ("r", 8, 5), ("r", 8, 7), ("r", 8,
    3), ("r", 8, 2), ("r", 8, 4), ("r", 8, 6), ("m", 8), ("m", 7),
)
DXS = (2, 1, 3, 0)


def below(s):
    return 2 * s - 1 if s else 0


def above(s):
    return 2 * s


def pair(s):
    if s == 0:
        return 0, 1
    return (2 * s - 1, 2) if s < FAR else (2 * FAR - 1, 1)


def join(v):
    lane = lax.broadcasted_iota(jnp.int32, (1, LANES), 1)
    middle = (lane >= ROWS) & (lane < 2 * ROWS)
    rows = [v[i] for i in range(v.shape[0])]
    top = rows[0]
    for r in rows[1:]:
        top = jnp.maximum(top, r)
    total = jnp.zeros_like(top)
    for r in rows:
        scale = pltpu.roll(jnp.exp(r - top), ROWS, 1)
        total = total + r * jnp.where(middle, scale, 1.0)
    return jnp.where(lane < ROWS, top, total)


def kernel(hidden, weight, shares, targets, out,
           X, W, acc, part, spare, goal, own_sh, pack, sxy, sz, sc,
           out_sem, zr, ar, rr, orr, vr, fr, ws, wr, wl, hl, gl, ps, pr,
           xs, xr, ts, tr, cs, cr):
    pipe = lax.axis_index("pipe")
    tensor = lax.axis_index("tensor")
    x, y = pipe // NY, pipe % NY
    z, c = tensor // 2, tensor % 2

    def at_xy(dx, dy):
        return (((x + dx) % NX) * NY + (y + dy) % NY, tensor)

    def at_z(d):
        return (pipe, ((z + d) % NZ) * 2 + c)

    sibling = (pipe, z * 2 + 1 - c)
    sent = []

    def send(src, dst, recv_sem, device):
        pltpu.make_async_remote_copy(
            src_ref=src, dst_ref=dst, send_sem=out_sem, recv_sem=recv_sem,
            device_id=device, device_id_type=MESH).start()
        sent.append(math.prod(src.shape))

    def arrived(ref, sem):
        pltpu.make_async_copy(ref, ref, sem).wait()

    def feature_block(j, core):
        step = (j + 1) // 2
        at = jnp.where(j % 2 == 1, z + NZ - step, z + step) % NZ
        return pl.ds(pl.multiple_of((2 * at + core) * WIDTH, WIDTH), WIDTH)

    def own_weight(j):
        return pltpu.make_async_copy(
            weight.at[:, feature_block(j, c)], W.at[j, pl.ds(0, SLOTS), :], wl)

    def other_weight(j):
        return pltpu.make_async_remote_copy(
            src_ref=weight.at[:, feature_block(j, 1 - c)],
            dst_ref=W.at[j, pl.ds(SLOTS, SLOTS), :],
            send_sem=ws, recv_sem=wr, device_id=sibling, device_id_type=MESH)

    barrier = pltpu.get_barrier_semaphore()
    greet = [at_xy(1, 0), at_xy(3, 0), at_xy(0, 1), at_xy(0, 3), at_z(1), at_z(15),
             at_xy(2, 0), at_xy(0, 2), sibling]
    for device in greet:
        pl.semaphore_signal(barrier, inc=1, device_id=device, device_id_type=MESH)
    own_block = pltpu.make_async_copy(hidden, X.at[0, 0, 0], hl)
    own_block.start()
    pl.semaphore_wait(barrier, len(greet))

    wide, narrow = pl.ds(0, WIDE), pl.ds(WIDE, WIDTH - WIDE)
    upper, lower = pl.ds(0, HALF), pl.ds(HALF, HALF)
    both = pl.ds(0, ROWS)

    def z_send(s):
        hop = HOP[s - 1]
        if s == hop:
            src_up = src_down = hidden.at[:, wide]
        else:
            src_up, src_down = X.at[below(s - hop), 0, 0, :, wide], X.at[above(s - hop), 0, 0, :, wide]
        dst_up, dst_down = X.at[below(s), 0, 0, :, wide], X.at[min(above(s), NZ - 1), 0, 0, :, wide]
        if s == FAR:
            src_up, dst_up = src_up.at[upper], dst_up.at[upper]
            src_down, dst_down = src_down.at[lower], dst_down.at[lower]
        send(src_up, dst_up, zr.at[s - 1], at_z(hop))
        send(src_down, dst_down, zr.at[s - 1], at_z(NZ - hop))

    def blocks(n):
        return X.at[pl.ds(0, n), 0, 0, :, wide]

    def strips(a, b):
        return X.at[0, pl.ds(0, a), pl.ds(0, b), :, narrow]

    def z_wait(s):
        arrived(blocks(2 if s < FAR else 1), zr.at[s - 1])

    def o_send(s):
        first, n = pair(s)
        at = pl.ds(first, n)
        if s == 0:
            def src(r):
                return hidden.at[r, wide]

            def dst(a, b, r):
                return X.at[0, a, b, r, wide]
        else:
            def src(r):
                return X.at[at, 0, 0, r, wide]

            def dst(a, b, r):
                return X.at[at, a, b, r, wide]
        plan = [((1, 0), both), ((0, 1), both), ((3, 0), both), ((0, 3), both), ((2, 0), upper), ((0, 2), lower)]
        for (dx, dy), r in plan:
            send(src(r), dst(-dx % NX, -dy % NY, r), orr.at[s], at_xy(dx, dy))

    def o_wait(s):
        arrived(blocks(5 * pair(s)[1]), orr.at[s])

    def v_send(s):
        at, rest = pl.ds(*pair(s)), pl.ds(1, 3)
        for d in (1, 3):
            send(X.at[at, rest, 0, upper, wide], X.at[at, rest, -d % NY, upper, wide],
                 vr.at[s], at_xy(0, d))
            send(X.at[at, 0, rest, lower, wide], X.at[at, -d % NX, rest, lower, wide],
                 vr.at[s], at_xy(d, 0))

    def v_wait(s):
        arrived(blocks(6 * pair(s)[1]), vr.at[s])

    def f_send(s):
        at = pl.ds(*pair(s))
        for i, d in enumerate((1, 3)):
            h = pl.ds(2 * i, 2)
            send(X.at[at, h, -d % NY, upper, wide], X.at[at, h, 2, upper, wide],
                 fr.at[s], at_xy(0, d))
            send(X.at[at, -d % NX, h, lower, wide], X.at[at, 2, h, lower, wide],
                 fr.at[s], at_xy(d, 0))

    def f_wait(s):
        arrived(blocks(4 * pair(s)[1]), fr.at[s])

    def a1_send():
        for d in (1, 3, 2):
            send(hidden.at[:, narrow], X.at[0, -d % NX, 0, :, narrow], ar.at[1], at_xy(d, 0))

    def a0_send():
        for d in (1, 3, 2):
            send(hidden.at[:, narrow], X.at[0, 0, -d % NY, :, narrow], ar.at[0], at_xy(0, d))

    def a0_wait():
        arrived(strips(1, 3), ar.at[0])

    def a2_send():
        arrived(strips(1, 3), ar.at[1])
        rest = pl.ds(1, 3)
        for d in (1, 3, 2):
            send(X.at[0, rest, 0, :, narrow], X.at[0, rest, -d % NY, :, narrow], ar.at[2], at_xy(0, d))

    def a2_wait():
        arrived(strips(3, 3), ar.at[2])

    def slab(j, h):
        if PIECES == NX:
            return X.at[j, pl.ds(h, 1), :, :, narrow]
        return X.at[j, pl.ds(h // 2, 1), pl.ds(2 * (h % 2), 2), :, narrow]

    def ring_send(s, h):
        if s < FAR or h < PIECES // 2:
            send(slab(below(s - 1), h), slab(below(s), h), rr.at[s - 1, h], at_z(1))
        if s < FAR or h >= PIECES // 2:
            send(slab(above(s - 1), h), slab(min(above(s), NZ - 1), h), rr.at[s - 1, h], at_z(NZ - 1))

    def ring_wait(s, h):
        n = NX * NY // PIECES * (2 if s < FAR else 1)
        arrived(strips(n // min(n, NY), min(n, NY)), rr.at[s - 1, h])

    def multiply(s):
        first, n = pair(s)
        if s == 0:
            arrived(W.at[:, pl.ds(0, SLOTS), :], wl)
            arrived(W.at[:, pl.ds(SLOTS, SLOTS), :], wr)

        @pl.loop(first, first + n)
        def _(j):
            part_sum = lax.dot_general(
                W[j], X[j].reshape(NX * NY * ROWS, WIDTH),
                (((1,), (1,)), ((), ())), preferred_element_type=jnp.float32)
            if s == 0:
                acc[...] = part_sum
            else:
                acc[...] += part_sum

    def all_left():
        assert sum(sent) == math.prod(X.shape) - ROWS * WIDTH
        arrived(X, out_sem)
        arrived(W.at[:, pl.ds(SLOTS, SLOTS), :], ws)

    for t in range(1, FAR + 1):
        if t == HOP[t - 1]:
            z_send(t)
    o_send(0)
    a1_send()
    a0_send()

    @pl.loop(0, NZ)
    def _(j):
        other_weight(j).start()
        own_weight(j).start()

    goals = [pltpu.make_async_copy(targets.at[(x + d) % NX], goal.at[d], gl.at[0]) for d in range(NX)]
    share_copy = pltpu.make_async_copy(shares, own_sh, gl.at[1])
    for g in goals + [share_copy]:
        g.start()
    pltpu.make_async_copy(hidden, spare, out_sem).start()

    def event(kind, s=0, h=0):
        if kind == "z":
            z_wait(s)
            for t in range(s + 1, FAR + 1):
                if t - HOP[t - 1] == s:
                    z_send(t)
            o_send(s)
        elif kind == "o":
            o_wait(s)
            v_send(s)
        elif kind == "v":
            v_wait(s)
            f_send(s)
        elif kind == "m":
            f_wait(s)
            multiply(s)
        elif kind == "a0":
            a0_wait()
            for h in range(PIECES // NX):
                ring_send(1, h)
        elif kind == "a2":
            a2_send()
        elif kind == "a3":
            a2_wait()
            for h in range(PIECES // NX, PIECES):
                ring_send(1, h)
        else:
            ring_wait(s, h)
            if s < FAR:
                ring_send(s + 1, h)

    own_block.wait()
    for name in ORDER:
        event(*name)

    def row_send(src, dst, send_sem, recv_sem, device):
        pltpu.make_async_remote_copy(
            src_ref=src, dst_ref=dst, send_sem=send_sem, recv_sem=recv_sem,
            device_id=device, device_id_type=MESH).start()

    def swap(dx):
        cols = pl.ds(dx * LANES, LANES)
        return pltpu.make_async_remote_copy(
            src_ref=acc.at[pl.ds(SLOTS, SLOTS), cols], dst_ref=part.at[:, cols],
            send_sem=ps, recv_sem=pr.at[dx], device_id=sibling, device_id_type=MESH)

    for dx in DXS:
        swap(dx).start()
    arrived(goal, gl.at[0])
    share_copy.wait()
    own_share = jnp.int32(0)
    offset = jnp.int32(0)
    for s in range(NX * NY):
        own_share = own_share + jnp.where(s == pipe, own_sh[s], 0)
        offset = offset + jnp.where(s < pipe, own_sh[s], 0)
    position = lax.broadcasted_iota(jnp.int32, (SLOTS, 1), 0) * (2 * NZ) + tensor
    live = position < own_share
    word = position + offset
    lane = lax.broadcasted_iota(jnp.int32, (1, LANES), 1)

    def packed(values, dy):
        top, total, pick = values
        moved = [pltpu.roll(v, (ROWS * (i - dy)) % LANES, 1) if (ROWS * (i - dy)) % LANES else v
                 for i, v in enumerate((top, total, pick))]
        return jnp.where(lane < ROWS, moved[0], jnp.where(lane < 2 * ROWS, moved[1], moved[2]))

    for dx in DXS:
        cols = pl.ds(dx * LANES, LANES)
        swap(dx).wait_recv()
        logits = acc[pl.ds(0, SLOTS), cols] + part[:, cols]
        want = goal[dx]
        turned = want
        for k in range(1, NY):
            turned = jnp.where(y == k, pltpu.roll(want, LANES - ROWS * k, 1), turned)
        top = jnp.max(jnp.where(live, logits, VERY_NEGATIVE), axis=0, keepdims=True)
        total = jnp.sum(jnp.where(live, jnp.exp(logits - top), 0.0), axis=0, keepdims=True)
        pick = jnp.sum(jnp.where(live & (word == turned), logits, 0.0), axis=0, keepdims=True)
        for dy in DXS:
            row = packed((top, total, pick), dy)
            if dx == 0 and dy == 0:
                sxy[0] = row
            else:
                pack[dx * NY + dy] = row
                to = (-dx % NX) * NY + (-dy % NY)
                row_send(pack.at[dx * NY + dy], sxy.at[to], xs, xr, at_xy(dx, dy))
    arrived(sxy.at[pl.ds(1, NX * NY - 1)], xr)
    sz[z] = join(sxy[...])
    for d in (8, 7, 9, 6, 10, 5, 11, 4, 12, 3, 13, 2, 14, 1, 15):
        row_send(sz.at[z], sz.at[z], ts, tr, at_z(d))
    arrived(part, ps)
    all_left()
    arrived(sz.at[pl.ds(1, NZ - 1)], tr)
    sc[c] = join(sz[...])
    row_send(sc.at[c], sc.at[c], cs, cr, sibling)
    arrived(sc.at[1 - c], cr)
    row = join(sc[...])
    log_total = pltpu.roll(row, ROWS, 1) + jnp.log(jnp.where((lane >= ROWS) & (lane < 2 * ROWS), row, 1.0))
    out[...] = jnp.where(lane < ROWS, row, jnp.where(
        lane < 2 * ROWS, log_total, row - pltpu.roll(log_total, ROWS, 1)))
    arrived(sxy.at[pl.ds(1, NX * NY - 1)], xs)
    arrived(sz.at[pl.ds(1, NZ - 1)], ts)
    arrived(sc.at[0], cs)


def local(hidden, head_weight, shares, targets):
    dma = pltpu.SemaphoreType.DMA
    rows = NX * NY * ROWS
    n = FAR + 1
    line = lambda k: pltpu.VMEM((k, 1, LANES), jnp.float32)
    hbm = pl.BlockSpec(memory_space=pltpu.HBM)
    out = pl.pallas_call(
        kernel,
        out_shape=jax.ShapeDtypeStruct((1, LANES), jnp.float32),
        in_specs=[hbm] * 4,
        out_specs=pl.BlockSpec(memory_space=pltpu.VMEM),
        scratch_shapes=[
            pltpu.VMEM((NZ, NX, NY, ROWS, WIDTH), jnp.bfloat16),
            pltpu.VMEM((NZ, 2 * SLOTS, WIDTH), jnp.bfloat16),
            pltpu.VMEM((2 * SLOTS, rows), jnp.float32),
            pltpu.VMEM((SLOTS, rows), jnp.float32),
            pltpu.VMEM((ROWS, WIDTH), jnp.bfloat16),
            pltpu.VMEM((NX, 1, LANES), jnp.int32),
            pltpu.SMEM((NX * NY,), jnp.int32),
            line(16), line(16), line(NZ), line(2),
            dma(()), dma((FAR,)), dma((3,)), dma((FAR, PIECES)), dma((n,)), dma((n,)), dma((n,)),
            dma(()), dma(()), dma(()), dma(()), dma((2,)), dma(()), dma((NX,)),
            *[dma(()) for _ in range(6)],
        ],
        compiler_params=pltpu.CompilerParams(
            collective_id=0, has_side_effects=True, vmem_limit_bytes=60 * 1024 * 1024),
        cost_estimate=pl.CostEstimate(
            flops=2 * rows * SLOTS * 2 * NZ * WIDTH, bytes_accessed=22 * 1024 * 1024,
            transcendentals=rows * SLOTS),
    )(hidden, head_weight, shares, targets.reshape(NX, 1, LANES))
    return tuple(out[0, ROWS * i:ROWS * (i + 1)] for i in range(3))


def solution(mesh):
    in_specs = (P("pipe", "tensor"), P(("pipe", "tensor"), None), P(), P())
    out_specs = (P("pipe"), P("pipe"), P("pipe"))
    return jax.shard_map(local, mesh=mesh, in_specs=in_specs, out_specs=out_specs, check_vma=False)
```

time: 87.9 us -> 74.9 us (0.85)
  Pallas kernels: 85.8 us -> 72.8 us
    pallas_call x1, Pallas kernels: 85.8 us -> 72.8 us  [local(): pl.pallas_call(kernel, out_shape=jax.ShapeDtypeStruct((1, LANES), jnp.flo...]
where the time goes in v3:
time: 74.9 us; the launch traced here: 74.8 us
  Pallas kernels  72.8 us (97%)
  local copies, waits for them, and re-layouts  1.3 us (2%)
    pallas_call x1, Pallas kernels, local(): pl.pallas_call(kernel, out_shape=jax.ShapeDtypeStruct((1, LANES), jnp.flo...  72.8 us

profile of v3, /device:TPU:1, one launch (start us, length us, event | category | flops | bytes accessed | tf_op | source)
XLA Modules:
  0.0 74.8 jit_solution(7509364611205291535)
XLA Ops:
  0.6 72.8 %shard_map.67 = f32[1,128]{1,0:T(1,128)} custom-call(bf16[32,512]{1,0:T(8,128)(2,1)} %hidden.1, bf16[144,16384]{1,0:T(8,128)(2,1)} %weight.1, s32[16]{0:T(128)} %shares.1, s32[4,1,128]{2,1,0:T(1,128)} %bitcast.7), custom_call_target="tpu_custom_call" | custom-call | flops 2415919104 | bytes 23068672 | tf_op jit(solution)/shard_map/pallas_call | solution.py:373
  73.5 1.3 %slice_bitcast_fusion = (f32[32]{0:T(128)}, f32[32]{0:T(128)}, f32[32]{0:T(128)}) fusion(f32[1,128]{1,0:T(1,128)} %shard_map.67), kind=kLoop, calls=%fused_computation | loop fusion | bytes 768 | tf_op jit(solution)/shard_map/squeeze | solution.py:397

commit v4 on v3

--- a/solution.py
+++ b/solution.py
@@ -17,23 +17,24 @@
 SLOTS = 144
 LANES = 128
 MESH = pl.DeviceIdType.MESH
-HOP = (1, 1, 1, 1, 1, 1, 1, 1)
+HOP = (1,) * 8
 PIECES = 8
 ORDER = (
-    ("z", 1), ("a2",), ("a0",), ("o", 0), ("z", 2), ("r", 1, 1), ("r", 1, 0), ("o", 1), ("z", 3), ("a3",),
-    ("v", 0), ("r", 2, 1), ("r", 2, 0), ("o", 2), ("z", 4), ("m", 0), ("r", 1, 5), ("r", 1, 7), ("r", 1, 3),
-    ("r", 1, 2), ("r", 1, 4), ("r", 1, 6), ("r", 3, 1), ("r", 3, 0), ("o", 3), ("v", 1), ("z", 5), ("v", 2),
-    ("o", 4), ("r", 2, 5), ("r", 2, 7), ("r", 2, 3), ("r", 2, 2), ("r", 2, 4), ("r", 2, 6), ("r", 4, 1), ("r",
-    4, 0), ("z", 6), ("r", 3, 5), ("r", 3, 7), ("r", 3, 3), ("m", 1), ("r", 3, 2), ("o", 5), ("r", 3, 4),
-    ("v", 3), ("r", 3, 6), ("r", 5, 1), ("r", 5, 0), ("r", 4, 5), ("z", 7), ("r", 4, 7), ("r", 4, 3), ("m",
-    2), ("o", 6), ("v", 4), ("r", 4, 2), ("r", 4, 4), ("r", 4, 6), ("r", 6, 1), ("r", 6, 0), ("z", 8), ("r",
-    5, 5), ("r", 5, 7), ("r", 5, 3), ("r", 5, 2), ("r", 5, 4), ("m", 3), ("r", 5, 6), ("v", 5), ("r", 7, 1),
-    ("o", 7), ("r", 7, 0), ("r", 6, 5), ("r", 6, 7), ("r", 6, 3), ("o", 8), ("r", 6, 2), ("r", 6, 4), ("m",
-    4), ("v", 6), ("r", 6, 6), ("r", 8, 1), ("r", 8, 0), ("m", 5), ("r", 7, 5), ("r", 7, 7), ("r", 7, 3),
-    ("v", 7), ("r", 7, 2), ("r", 7, 4), ("v", 8), ("r", 7, 6), ("m", 6), ("r", 8, 5), ("r", 8, 7), ("r", 8,
-    3), ("r", 8, 2), ("r", 8, 4), ("r", 8, 6), ("m", 8), ("m", 7),
+    ("z", 1), ("a0",), ("a2",), ("o", 0), ("z", 2), ("r", 1, 0), ("r", 1, 1), ("o", 1), ("v", 0), ("a3",),
+    ("z", 3), ("r", 2, 0), ("r", 2, 1), ("o", 2), ("v", 1), ("m", 0), ("r", 1, 7), ("r", 1, 6), ("r", 1, 2),
+    ("r", 1, 4), ("r", 1, 3), ("r", 1, 5), ("o", 3), ("r", 3, 0), ("r", 3, 1), ("z", 4), ("v", 2), ("r", 2,
+    7), ("r", 2, 6), ("r", 2, 2), ("r", 2, 4), ("r", 2, 3), ("r", 2, 5), ("r", 4, 0), ("r", 4, 1), ("m", 1),
+    ("z", 5), ("r", 3, 7), ("r", 3, 6), ("r", 3, 2), ("v", 3), ("r", 3, 4), ("r", 3, 3), ("o", 4), ("r", 3,
+    5), ("r", 5, 0), ("r", 5, 1), ("z", 6), ("r", 4, 7), ("r", 4, 6), ("r", 4, 2), ("o", 5), ("r", 4, 4),
+    ("r", 4, 3), ("r", 4, 5), ("r", 6, 0), ("r", 6, 1), ("m", 2), ("z", 7), ("r", 5, 7), ("r", 5, 6), ("v",
+    4), ("r", 5, 2), ("r", 5, 4), ("r", 5, 3), ("o", 6), ("r", 5, 5), ("r", 7, 0), ("r", 7, 1), ("v", 5),
+    ("z", 8), ("r", 6, 7), ("r", 6, 6), ("r", 6, 2), ("o", 7), ("r", 6, 4), ("r", 6, 3), ("r", 6, 5), ("r", 8,
+    0), ("r", 8, 1), ("m", 3), ("r", 7, 7), ("r", 7, 6), ("v", 6), ("r", 7, 2), ("o", 8), ("r", 7, 4), ("r",
+    7, 3), ("r", 7, 5), ("v", 7), ("m", 4), ("r", 8, 7), ("r", 8, 6), ("r", 8, 2), ("r", 8, 4), ("r", 8, 3),
+    ("v", 8), ("r", 8, 5), ("m", 5), ("m", 6), ("m", 7), ("m", 8),
 )
-DXS = (2, 1, 3, 0)
+DXS = (2, 3, 1, 0)
+LAST = (8,)
 
 
 def below(s):
@@ -65,9 +66,9 @@
 
 
 def kernel(hidden, weight, shares, targets, out,
-           X, W, acc, part, spare, goal, own_sh, pack, sxy, sz, sc,
+           X, W, acc, part, spare, goal, own_sh, pack, sxy, sz,
            out_sem, zr, ar, rr, orr, vr, fr, ws, wr, wl, hl, gl, ps, pr,
-           xs, xr, ts, tr, cs, cr):
+           xs, xr, ts, tr):
     pipe = lax.axis_index("pipe")
     tensor = lax.axis_index("tensor")
     x, y = pipe // NY, pipe % NY
@@ -221,6 +222,37 @@
         n = NX * NY // PIECES * (2 if s < FAR else 1)
         arrived(strips(n // min(n, NY), min(n, NY)), rr.at[s - 1, h])
 
+    def row_send(src, dst, send_sem, recv_sem, device):
+        pltpu.make_async_remote_copy(
+            src_ref=src, dst_ref=dst, send_sem=send_sem, recv_sem=recv_sem,
+            device_id=device, device_id_type=MESH).start()
+
+    def swap(dx):
+        cols = pl.ds(dx * LANES, LANES)
+        return pltpu.make_async_remote_copy(
+            src_ref=acc.at[pl.ds(SLOTS, SLOTS), cols], dst_ref=part.at[:, cols],
+            send_sem=ps, recv_sem=pr.at[dx], device_id=sibling, device_id_type=MESH)
+
+    def multiply_last():
+        first, n = pair(LAST[0])[0], sum(pair(s)[1] for s in LAST)
+
+        def add(slots, x0):
+            cols = pl.ds(x0 * LANES, 2 * LANES)
+            total = acc[slots, cols]
+            for j in range(first, first + n):
+                total += lax.dot_general(
+                    W[j, slots, :], X[j, pl.ds(x0, 2)].reshape(2 * NY * ROWS, WIDTH),
+                    (((1,), (1,)), ((), ())), preferred_element_type=jnp.float32)
+            acc[slots, cols] = total
+
+        for x0 in (2, 0):
+            add(pl.ds(SLOTS, SLOTS), x0)
+            for dx in DXS:
+                if dx // 2 == x0 // 2:
+                    swap(dx).start()
+        for x0 in (2, 0):
+            add(pl.ds(0, SLOTS), x0)
+
     def multiply(s):
         first, n = pair(s)
         if s == 0:
@@ -259,6 +291,24 @@
     for g in goals + [share_copy]:
         g.start()
     pltpu.make_async_copy(hidden, spare, out_sem).start()
+
+    known = {}
+
+    def prepare():
+        arrived(goal, gl.at[0])
+        share_copy.wait()
+        own_share = jnp.int32(0)
+        offset = jnp.int32(0)
+        for s in range(NX * NY):
+            own_share = own_share + jnp.where(s == pipe, own_sh[s], 0)
+            offset = offset + jnp.where(s < pipe, own_sh[s], 0)
+        known["share"] = own_share
+        for dx in range(NX):
+            want = goal[dx] - offset
+            turned = want
+            for k in range(1, NY):
+                turned = jnp.where(y == k, pltpu.roll(want, LANES - ROWS * k, 1), turned)
+            goal[dx] = turned
 
     def event(kind, s=0, h=0):
         if kind == "z":
@@ -275,7 +325,8 @@
             f_send(s)
         elif kind == "m":
             f_wait(s)
-            multiply(s)
+            if s not in LAST:
+                multiply(s)
         elif kind == "a0":
             a0_wait()
             for h in range(PIECES // NX):
@@ -294,30 +345,10 @@
     own_block.wait()
     for name in ORDER:
         event(*name)
-
-    def row_send(src, dst, send_sem, recv_sem, device):
-        pltpu.make_async_remote_copy(
-            src_ref=src, dst_ref=dst, send_sem=send_sem, recv_sem=recv_sem,
-            device_id=device, device_id_type=MESH).start()
-
-    def swap(dx):
-        cols = pl.ds(dx * LANES, LANES)
-        return pltpu.make_async_remote_copy(
-            src_ref=acc.at[pl.ds(SLOTS, SLOTS), cols], dst_ref=part.at[:, cols],
-            send_sem=ps, recv_sem=pr.at[dx], device_id=sibling, device_id_type=MESH)
-
-    for dx in DXS:
-        swap(dx).start()
-    arrived(goal, gl.at[0])
-    share_copy.wait()
-    own_share = jnp.int32(0)
-    offset = jnp.int32(0)
-    for s in range(NX * NY):
-        own_share = own_share + jnp.where(s == pipe, own_sh[s], 0)
-        offset = offset + jnp.where(s < pipe, own_sh[s], 0)
-    position = lax.broadcasted_iota(jnp.int32, (SLOTS, 1), 0) * (2 * NZ) + tensor
-    live = position < own_share
-    word = position + offset
+        if name == ("m", 0):
+            prepare()
+    multiply_last()
+
     lane = lax.broadcasted_iota(jnp.int32, (1, LANES), 1)
 
     def packed(values, dy):
@@ -326,42 +357,39 @@
                  for i, v in enumerate((top, total, pick))]
         return jnp.where(lane < ROWS, moved[0], jnp.where(lane < 2 * ROWS, moved[1], moved[2]))
 
+    position = lax.broadcasted_iota(jnp.int32, (SLOTS, LANES), 0) * (2 * NZ) + tensor
+    live = position < known["share"]
     for dx in DXS:
         cols = pl.ds(dx * LANES, LANES)
         swap(dx).wait_recv()
         logits = acc[pl.ds(0, SLOTS), cols] + part[:, cols]
-        want = goal[dx]
-        turned = want
-        for k in range(1, NY):
-            turned = jnp.where(y == k, pltpu.roll(want, LANES - ROWS * k, 1), turned)
         top = jnp.max(jnp.where(live, logits, VERY_NEGATIVE), axis=0, keepdims=True)
         total = jnp.sum(jnp.where(live, jnp.exp(logits - top), 0.0), axis=0, keepdims=True)
-        pick = jnp.sum(jnp.where(live & (word == turned), logits, 0.0), axis=0, keepdims=True)
+        pick = jnp.sum(jnp.where(live & (position == goal[dx]), logits, 0.0), axis=0, keepdims=True)
         for dy in DXS:
             row = packed((top, total, pick), dy)
+            to = c * NX * NY + (-dx % NX) * NY + (-dy % NY)
             if dx == 0 and dy == 0:
-                sxy[0] = row
+                sxy[to] = row
+                row_send(sxy.at[to], sxy.at[to], xs, xr, sibling)
             else:
                 pack[dx * NY + dy] = row
-                to = (-dx % NX) * NY + (-dy % NY)
-                row_send(pack.at[dx * NY + dy], sxy.at[to], xs, xr, at_xy(dx, dy))
-    arrived(sxy.at[pl.ds(1, NX * NY - 1)], xr)
+                for core in range(2):
+                    device = (at_xy(dx, dy)[0], z * 2 + core)
+                    row_send(pack.at[dx * NY + dy], sxy.at[to], xs, xr, device)
+    arrived(sxy.at[pl.ds(1, 2 * NX * NY - 1)], xr)
     sz[z] = join(sxy[...])
     for d in (8, 7, 9, 6, 10, 5, 11, 4, 12, 3, 13, 2, 14, 1, 15):
         row_send(sz.at[z], sz.at[z], ts, tr, at_z(d))
     arrived(part, ps)
     all_left()
     arrived(sz.at[pl.ds(1, NZ - 1)], tr)
-    sc[c] = join(sz[...])
-    row_send(sc.at[c], sc.at[c], cs, cr, sibling)
-    arrived(sc.at[1 - c], cr)
-    row = join(sc[...])
+    row = join(sz[...])
     log_total = pltpu.roll(row, ROWS, 1) + jnp.log(jnp.where((lane >= ROWS) & (lane < 2 * ROWS), row, 1.0))
     out[...] = jnp.where(lane < ROWS, row, jnp.where(
         lane < 2 * ROWS, log_total, row - pltpu.roll(log_total, ROWS, 1)))
-    arrived(sxy.at[pl.ds(1, NX * NY - 1)], xs)
+    arrived(sxy.at[pl.ds(1, 2 * NX * NY - 1)], xs)
     arrived(sz.at[pl.ds(1, NZ - 1)], ts)
-    arrived(sc.at[0], cs)
 
 
 def local(hidden, head_weight, shares, targets):
@@ -383,10 +411,10 @@
             pltpu.VMEM((ROWS, WIDTH), jnp.bfloat16),
             pltpu.VMEM((NX, 1, LANES), jnp.int32),
             pltpu.SMEM((NX * NY,), jnp.int32),
-            line(16), line(16), line(NZ), line(2),
+            line(NX * NY), line(2 * NX * NY), line(NZ),
             dma(()), dma((FAR,)), dma((3,)), dma((FAR, PIECES)), dma((n,)), dma((n,)), dma((n,)),
             dma(()), dma(()), dma(()), dma(()), dma((2,)), dma(()), dma((NX,)),
-            *[dma(()) for _ in range(6)],
+            *[dma(()) for _ in range(4)],
         ],
         compiler_params=pltpu.CompilerParams(
             collective_id=0, has_side_effects=True, vmem_limit_bytes=60 * 1024 * 1024),

time: 74.9 us -> 74.1 us (0.989)
  Pallas kernels: 72.8 us -> 72 us
    pallas_call x1, Pallas kernels: 72.8 us -> 72 us  [local(): pl.pallas_call(kernel, out_shape=jax.ShapeDtypeStruct((1, LANES), jnp.flo...]
where the time goes in v4:
time: 74.1 us; the launch traced here: 73.9 us
  Pallas kernels  72 us (97%)
  local copies, waits for them, and re-layouts  1.3 us (2%)
    pallas_call x1, Pallas kernels, local(): pl.pallas_call(kernel, out_shape=jax.ShapeDtypeStruct((1, LANES), jnp.flo...  72 us

profile of v4, /device:TPU:1, one launch (start us, length us, event | category | flops | bytes accessed | tf_op | source)
XLA Modules:
  0.0 73.9 jit_solution(5838737564582976029)
XLA Ops:
  0.6 72.0 %shard_map.67 = f32[1,128]{1,0:T(1,128)} custom-call(bf16[32,512]{1,0:T(8,128)(2,1)} %hidden.1, bf16[144,16384]{1,0:T(8,128)(2,1)} %weight.1, s32[16]{0:T(128)} %shares.1, s32[4,1,128]{2,1,0:T(1,128)} %bitcast.7), custom_call_target="tpu_custom_call" | custom-call | flops 2415919104 | bytes 23068672 | tf_op jit(solution)/shard_map/pallas_call | solution.py:401
  72.6 1.3 %slice_bitcast_fusion = (f32[32]{0:T(128)}, f32[32]{0:T(128)}, f32[32]{0:T(128)}) fusion(f32[1,128]{1,0:T(1,128)} %shard_map.67), kind=kLoop, calls=%fused_computation | loop fusion | bytes 768 | tf_op jit(solution)/shard_map/squeeze | solution.py:425

commit v5 on v4

--- a/solution.py
+++ b/solution.py
@@ -18,20 +18,17 @@
 LANES = 128
 MESH = pl.DeviceIdType.MESH
 HOP = (1,) * 8
-PIECES = 8
+PIECES = 4
 ORDER = (
-    ("z", 1), ("a0",), ("a2",), ("o", 0), ("z", 2), ("r", 1, 0), ("r", 1, 1), ("o", 1), ("v", 0), ("a3",),
-    ("z", 3), ("r", 2, 0), ("r", 2, 1), ("o", 2), ("v", 1), ("m", 0), ("r", 1, 7), ("r", 1, 6), ("r", 1, 2),
-    ("r", 1, 4), ("r", 1, 3), ("r", 1, 5), ("o", 3), ("r", 3, 0), ("r", 3, 1), ("z", 4), ("v", 2), ("r", 2,
-    7), ("r", 2, 6), ("r", 2, 2), ("r", 2, 4), ("r", 2, 3), ("r", 2, 5), ("r", 4, 0), ("r", 4, 1), ("m", 1),
-    ("z", 5), ("r", 3, 7), ("r", 3, 6), ("r", 3, 2), ("v", 3), ("r", 3, 4), ("r", 3, 3), ("o", 4), ("r", 3,
-    5), ("r", 5, 0), ("r", 5, 1), ("z", 6), ("r", 4, 7), ("r", 4, 6), ("r", 4, 2), ("o", 5), ("r", 4, 4),
-    ("r", 4, 3), ("r", 4, 5), ("r", 6, 0), ("r", 6, 1), ("m", 2), ("z", 7), ("r", 5, 7), ("r", 5, 6), ("v",
-    4), ("r", 5, 2), ("r", 5, 4), ("r", 5, 3), ("o", 6), ("r", 5, 5), ("r", 7, 0), ("r", 7, 1), ("v", 5),
-    ("z", 8), ("r", 6, 7), ("r", 6, 6), ("r", 6, 2), ("o", 7), ("r", 6, 4), ("r", 6, 3), ("r", 6, 5), ("r", 8,
-    0), ("r", 8, 1), ("m", 3), ("r", 7, 7), ("r", 7, 6), ("v", 6), ("r", 7, 2), ("o", 8), ("r", 7, 4), ("r",
-    7, 3), ("r", 7, 5), ("v", 7), ("m", 4), ("r", 8, 7), ("r", 8, 6), ("r", 8, 2), ("r", 8, 4), ("r", 8, 3),
-    ("v", 8), ("r", 8, 5), ("m", 5), ("m", 6), ("m", 7), ("m", 8),
+    ("z", 1), ("a0",), ("a2",), ("o", 0), ("z", 2), ("r", 1, 0), ("o", 1), ("z", 3), ("v", 0), ("a3",), ("r",
+    2, 0), ("o", 2), ("z", 4), ("v", 1), ("m", 0, 0), ("o", 3), ("r", 1, 3), ("r", 1, 2), ("r", 1, 1), ("r",
+    3, 0), ("z", 5), ("v", 2), ("o", 4), ("m", 1, 0), ("r", 2, 3), ("m", 1, 1), ("r", 2, 2), ("z", 6), ("r",
+    2, 1), ("r", 4, 0), ("o", 5), ("v", 3), ("r", 3, 3), ("m", 2, 0), ("m", 2, 1), ("r", 3, 2), ("z", 7),
+    ("v", 4), ("r", 3, 1), ("r", 5, 0), ("r", 4, 3), ("o", 6), ("m", 3, 0), ("z", 8), ("r", 4, 2), ("m", 3,
+    1), ("v", 5), ("r", 4, 1), ("r", 6, 0), ("r", 5, 3), ("o", 7), ("m", 4, 0), ("r", 5, 2), ("m", 4, 1),
+    ("o", 8), ("r", 5, 1), ("v", 6), ("m", 5, 0), ("r", 7, 0), ("r", 6, 3), ("m", 5, 1), ("r", 6, 2), ("v",
+    7), ("v", 8), ("r", 6, 1), ("m", 6, 0), ("m", 6, 1), ("r", 8, 0), ("r", 7, 3), ("r", 7, 2), ("r", 7, 1),
+    ("m", 7, 0), ("m", 7, 1), ("r", 8, 3), ("r", 8, 2), ("r", 8, 1), ("m", 8, 0),
 )
 DXS = (2, 3, 1, 0)
 LAST = (8,)
@@ -253,21 +250,18 @@
         for x0 in (2, 0):
             add(pl.ds(0, SLOTS), x0)
 
-    def multiply(s):
-        first, n = pair(s)
+    def multiply(s, h):
         if s == 0:
             arrived(W.at[:, pl.ds(0, SLOTS), :], wl)
             arrived(W.at[:, pl.ds(SLOTS, SLOTS), :], wr)
-
-        @pl.loop(first, first + n)
-        def _(j):
-            part_sum = lax.dot_general(
-                W[j], X[j].reshape(NX * NY * ROWS, WIDTH),
-                (((1,), (1,)), ((), ())), preferred_element_type=jnp.float32)
-            if s == 0:
-                acc[...] = part_sum
-            else:
-                acc[...] += part_sum
+        j = pair(s)[0] + h
+        product = lax.dot_general(
+            W[j], X[j].reshape(NX * NY * ROWS, WIDTH),
+            (((1,), (1,)), ((), ())), preferred_element_type=jnp.float32)
+        if s == 0:
+            acc[...] = product
+        else:
+            acc[...] += product
 
     def all_left():
         assert sum(sent) == math.prod(X.shape) - ROWS * WIDTH
@@ -281,10 +275,11 @@
     a1_send()
     a0_send()
 
-    @pl.loop(0, NZ)
-    def _(j):
-        other_weight(j).start()
-        own_weight(j).start()
+    def weights():
+        @pl.loop(0, NZ)
+        def _(j):
+            other_weight(j).start()
+            own_weight(j).start()
 
     goals = [pltpu.make_async_copy(targets.at[(x + d) % NX], goal.at[d], gl.at[0]) for d in range(NX)]
     share_copy = pltpu.make_async_copy(shares, own_sh, gl.at[1])
@@ -324,9 +319,10 @@
             v_wait(s)
             f_send(s)
         elif kind == "m":
-            f_wait(s)
+            if h == 0:
+                f_wait(s)
             if s not in LAST:
-                multiply(s)
+                multiply(s, h)
         elif kind == "a0":
             a0_wait()
             for h in range(PIECES // NX):
@@ -343,9 +339,11 @@
                 ring_send(s + 1, h)
 
     own_block.wait()
-    for name in ORDER:
+    for number, name in enumerate(ORDER, 1):
         event(*name)
-        if name == ("m", 0):
+        if number == 2:
+            weights()
+        if name == ("m", 0, 0):
             prepare()
     multiply_last()
 

time: 74.1 us -> 75.9 us (1.024)
  Pallas kernels: 72 us -> 73.8 us
    pallas_call x1, Pallas kernels: 72 us -> 73.8 us  [local(): pl.pallas_call(kernel, out_shape=jax.ShapeDtypeStruct((1, LANES), jnp.flo...]
where the time goes in v5:
time: 75.9 us; the launch traced here: 75.8 us
  Pallas kernels  73.8 us (97%)
  local copies, waits for them, and re-layouts  1.3 us (2%)
    pallas_call x1, Pallas kernels, local(): pl.pallas_call(kernel, out_shape=jax.ShapeDtypeStruct((1, LANES), jnp.flo...  73.8 us

profile of v5, /device:TPU:1, one launch (start us, length us, event | category | flops | bytes accessed | tf_op | source)
XLA Modules:
  0.0 75.8 jit_solution(3429795442719541169)
XLA Ops:
  0.6 73.8 %shard_map.67 = f32[1,128]{1,0:T(1,128)} custom-call(bf16[32,512]{1,0:T(8,128)(2,1)} %hidden.1, bf16[144,16384]{1,0:T(8,128)(2,1)} %weight.1, s32[16]{0:T(128)} %shares.1, s32[4,1,128]{2,1,0:T(1,128)} %bitcast.7), custom_call_target="tpu_custom_call" | custom-call | flops 2415919104 | bytes 23068672 | tf_op jit(solution)/shard_map/pallas_call | solution.py:399
  74.5 1.3 %slice_bitcast_fusion = (f32[32]{0:T(128)}, f32[32]{0:T(128)}, f32[32]{0:T(128)}) fusion(f32[1,128]{1,0:T(1,128)} %shard_map.67), kind=kLoop, calls=%fused_computation | loop fusion | bytes 768 | tf_op jit(solution)/shard_map/squeeze | solution.py:423

commit v6 on v4

--- a/solution.py
+++ b/solution.py
@@ -20,18 +20,18 @@
 HOP = (1,) * 8
 PIECES = 8
 ORDER = (
-    ("z", 1), ("a0",), ("a2",), ("o", 0), ("z", 2), ("r", 1, 0), ("r", 1, 1), ("o", 1), ("v", 0), ("a3",),
-    ("z", 3), ("r", 2, 0), ("r", 2, 1), ("o", 2), ("v", 1), ("m", 0), ("r", 1, 7), ("r", 1, 6), ("r", 1, 2),
-    ("r", 1, 4), ("r", 1, 3), ("r", 1, 5), ("o", 3), ("r", 3, 0), ("r", 3, 1), ("z", 4), ("v", 2), ("r", 2,
-    7), ("r", 2, 6), ("r", 2, 2), ("r", 2, 4), ("r", 2, 3), ("r", 2, 5), ("r", 4, 0), ("r", 4, 1), ("m", 1),
-    ("z", 5), ("r", 3, 7), ("r", 3, 6), ("r", 3, 2), ("v", 3), ("r", 3, 4), ("r", 3, 3), ("o", 4), ("r", 3,
-    5), ("r", 5, 0), ("r", 5, 1), ("z", 6), ("r", 4, 7), ("r", 4, 6), ("r", 4, 2), ("o", 5), ("r", 4, 4),
-    ("r", 4, 3), ("r", 4, 5), ("r", 6, 0), ("r", 6, 1), ("m", 2), ("z", 7), ("r", 5, 7), ("r", 5, 6), ("v",
-    4), ("r", 5, 2), ("r", 5, 4), ("r", 5, 3), ("o", 6), ("r", 5, 5), ("r", 7, 0), ("r", 7, 1), ("v", 5),
-    ("z", 8), ("r", 6, 7), ("r", 6, 6), ("r", 6, 2), ("o", 7), ("r", 6, 4), ("r", 6, 3), ("r", 6, 5), ("r", 8,
-    0), ("r", 8, 1), ("m", 3), ("r", 7, 7), ("r", 7, 6), ("v", 6), ("r", 7, 2), ("o", 8), ("r", 7, 4), ("r",
-    7, 3), ("r", 7, 5), ("v", 7), ("m", 4), ("r", 8, 7), ("r", 8, 6), ("r", 8, 2), ("r", 8, 4), ("r", 8, 3),
-    ("v", 8), ("r", 8, 5), ("m", 5), ("m", 6), ("m", 7), ("m", 8),
+    ("z", 1), ("a2",), ("a0",), ("o", 0), ("z", 2), ("r", 1, 1), ("r", 1, 0), ("o", 1), ("a3",), ("z", 3),
+    ("v", 0), ("r", 2, 1), ("o", 2), ("r", 2, 0), ("r", 1, 6), ("r", 1, 5), ("r", 1, 7), ("r", 1, 3), ("r", 1,
+    2), ("r", 1, 4), ("v", 1), ("r", 3, 1), ("z", 4), ("r", 3, 0), ("o", 3), ("v", 2), ("r", 2, 6), ("m", 0),
+    ("r", 2, 5), ("r", 2, 7), ("r", 2, 3), ("r", 2, 2), ("r", 2, 4), ("r", 4, 1), ("r", 4, 0), ("z", 5), ("r",
+    3, 6), ("m", 1), ("r", 3, 5), ("r", 3, 7), ("r", 3, 3), ("r", 3, 2), ("o", 4), ("r", 3, 4), ("r", 5, 1),
+    ("r", 5, 0), ("z", 6), ("r", 4, 6), ("v", 3), ("m", 2), ("r", 4, 5), ("o", 5), ("r", 4, 7), ("r", 4, 3),
+    ("r", 4, 2), ("r", 4, 4), ("r", 6, 1), ("r", 6, 0), ("r", 5, 6), ("z", 7), ("v", 4), ("r", 5, 5), ("r", 5,
+    7), ("r", 5, 3), ("o", 6), ("r", 5, 2), ("m", 3), ("r", 5, 4), ("r", 7, 1), ("r", 7, 0), ("z", 8), ("r",
+    6, 6), ("r", 6, 5), ("r", 6, 7), ("v", 5), ("r", 6, 3), ("r", 6, 2), ("o", 7), ("m", 4), ("r", 6, 4),
+    ("r", 8, 1), ("r", 7, 6), ("v", 6), ("r", 7, 5), ("r", 7, 7), ("o", 8), ("r", 7, 3), ("r", 7, 2), ("r", 8,
+    0), ("m", 5), ("r", 7, 4), ("v", 7), ("r", 8, 6), ("r", 8, 5), ("r", 8, 7), ("m", 6), ("v", 8), ("r", 8,
+    3), ("r", 8, 2), ("r", 8, 4), ("m", 7), ("m", 8),
 )
 DXS = (2, 3, 1, 0)
 LAST = (8,)

time: 74.1 us -> 73.4 us (level)
  no operation moved by 1% of the time
where the time goes in v6:
time: 73.4 us; the launch traced here: 73.2 us
  Pallas kernels  71.3 us (97%)
  local copies, waits for them, and re-layouts  1.3 us (2%)
    pallas_call x1, Pallas kernels, local(): pl.pallas_call(kernel, out_shape=jax.ShapeDtypeStruct((1, LANES), jnp.flo...  71.3 us

profile of v6, /device:TPU:1, one launch (start us, length us, event | category | flops | bytes accessed | tf_op | source)
XLA Modules:
  0.0 73.2 jit_solution(15864530905138773712)
XLA Ops:
  0.6 71.3 %shard_map.67 = f32[1,128]{1,0:T(1,128)} custom-call(bf16[32,512]{1,0:T(8,128)(2,1)} %hidden.1, bf16[144,16384]{1,0:T(8,128)(2,1)} %weight.1, s32[16]{0:T(128)} %shares.1, s32[4,1,128]{2,1,0:T(1,128)} %bitcast.7), custom_call_target="tpu_custom_call" | custom-call | flops 2415919104 | bytes 23068672 | tf_op jit(solution)/shard_map/pallas_call | solution.py:401
  71.9 1.3 %slice_bitcast_fusion = (f32[32]{0:T(128)}, f32[32]{0:T(128)}, f32[32]{0:T(128)}) fusion(f32[1,128]{1,0:T(1,128)} %shard_map.67), kind=kLoop, calls=%fused_computation | loop fusion | bytes 768 | tf_op jit(solution)/shard_map/squeeze | solution.py:425
